TPU v7x, 512 devices: a whole 4x8x8 slice. The times are simulated.
512 devices in a mesh: label: 64 (over y, x, core), query: 8 (over z).
Axes of the slice: x: 4, y: 8, z: 8, core: 2. Of those that a mesh axis runs over, the one named last changes fastest.
Arguments:
- queries: bfloat16 [1536, 768], P('query'), may hold values from -6 to 6
- label_ids: int32 [1536, 10], P('query'), may hold values from 0 to 4095, as said below
- label_text: bfloat16 [4096, 32, 768], P('label'), may hold values from -16 to 16
- up_weight: bfloat16 [768, 3072], P(None, 'query'), may hold values from -0.21875 to 0.21875
- down_weight: bfloat16 [768, 3072], P(None, 'query'), may hold values from -0.109375 to 0.109375
- free_vectors: float32 [4096, 768], P('label'), may hold values from -4 to 4
- moments: float32 [4096, 768], P('label'), may hold values from -0.06 to 0.06
- seconds: float32 [4096, 768], P('label'), may hold values from 1e-05 to 0.001
Outputs:
- free_new: float32 [4096, 768], P('label')
- moments_new: float32 [4096, 768], P('label')
- seconds_new: float32 [4096, 768], P('label')
- query_grad: float32 [1536, 768], P('query')
- up_grad: float32 [768, 3072], P('label', 'query')
- down_grad: float32 [768, 3072], P('label', 'query')
Inputs may be any that keep to these rules, and one draw needn't show every extreme that they name: `label_ids`: the 10 ids of one query are distinct.
All inputs are finite; a program needn't handle non-finite values.
Results may differ from a plain program's by a relative error of at most 0.023.
Values sent between devices are 32-bit elements; how exact they have to be, the bound alone decides.
A program may use at most 64 MiB of HBM per device.

v0:
```python
import jax
import jax.numpy as jnp
from jax import lax
from jax.sharding import PartitionSpec as P

beta_one = 0.9
beta_two = 0.999
adam_eps = 1e-08
learn_rate = 0.05
first_fix = 1.0 - 0.9**10
second_fix = 1.0 - 0.999**10


def gelu_tanh(values):
    return jax.nn.gelu(values, approximate=True)


def body(queries, label_ids, label_text, up_weight, down_weight, free_vectors, moments, seconds):
    label_rows, text_len, model_width = label_text.shape
    unit_cols = up_weight.shape[1]
    temper = 1.0 / jnp.sqrt(jnp.float32(model_width))
    text_rows = label_text.reshape(label_rows * text_len, model_width)
    preact = jnp.dot(text_rows, up_weight, preferred_element_type=jnp.float32)
    hidden = gelu_tanh(preact).astype(jnp.bfloat16)
    pooled_hidden = jnp.mean(
        hidden.reshape(label_rows, text_len, unit_cols), axis=1, dtype=jnp.float32
    )
    pooled_text = jnp.mean(label_text, axis=1, dtype=jnp.float32)
    encoded_part = jnp.einsum(
        "lf,df->ld", pooled_hidden, down_weight.astype(jnp.float32), precision=lax.Precision.HIGHEST
    )
    encoded = lax.psum(encoded_part, "query")
    label_vec = pooled_text + encoded + free_vectors
    label_bf = label_vec.astype(jnp.bfloat16)
    first_label = lax.axis_index("label") * label_rows
    local_ids = label_ids - first_label
    owners = (
        local_ids[:, :, None] == jnp.arange(label_rows, dtype=jnp.int32)[None, None, :]
    ).astype(jnp.float32)
    similar = jnp.einsum("id,jd->ij", queries, label_bf, preferred_element_type=jnp.float32)
    partial_value = jnp.einsum("ikj,ij->ik", owners, similar, precision=lax.Precision.HIGHEST)
    scores = lax.psum(partial_value, "label") * temper
    likely = jax.nn.softmax(scores, axis=-1)
    target = jnp.where(jnp.arange(scores.shape[1]) < 2, 0.5, 0.0).astype(jnp.float32)
    pair_coef = ((likely - target[None, :]) * temper).astype(jnp.bfloat16)
    spread = jnp.einsum(
        "ik,ikj->ij", pair_coef.astype(jnp.float32), owners, precision=lax.Precision.HIGHEST
    ).astype(jnp.bfloat16)
    query_terms = jnp.dot(spread, label_bf, preferred_element_type=jnp.float32)
    query_grad = lax.psum(query_terms, "label")
    grad_part = jnp.einsum("ij,id->jd", spread, queries, preferred_element_type=jnp.float32)
    count_part = jnp.sum(owners, axis=(0, 1))
    label_grad, counts = lax.psum((grad_part, count_part), "query")
    out_grad = label_grad.astype(jnp.bfloat16)
    hidden_grad = jnp.dot(out_grad, down_weight, preferred_element_type=jnp.float32) / text_len
    token_grad = jnp.broadcast_to(
        hidden_grad[:, None, :], (label_rows, text_len, unit_cols)
    ).reshape(label_rows * text_len, unit_cols)
    preact_grad = jax.vjp(gelu_tanh, preact)[1](token_grad)[0].astype(jnp.bfloat16)
    joined = lax.psum_scatter(
        jnp.concatenate(
            (
                lax.dot_general(
                    text_rows,
                    preact_grad,
                    (((0,), (0,)), ((), ())),
                    preferred_element_type=jnp.float32,
                ),
                jnp.einsum(
                    "ld,lf->df",
                    out_grad.astype(jnp.float32),
                    pooled_hidden,
                    precision=lax.Precision.HIGHEST,
                ),
            ),
            axis=1,
        ),
        "label",
        scatter_dimension=0,
        tiled=True,
    )
    up_part = joined[:, :unit_cols]
    down_part = joined[:, unit_cols:]
    touched = (counts > 0.5)[:, None]
    moment_step = beta_one * moments + (1.0 - beta_one) * label_grad
    second_step = beta_two * seconds + (1.0 - beta_two) * label_grad * label_grad
    update = (
        learn_rate * (moment_step / first_fix) / (jnp.sqrt(second_step / second_fix) + adam_eps)
    )
    free_new = jnp.where(touched, free_vectors - update, free_vectors)
    moments_new = jnp.where(touched, moment_step, moments)
    seconds_new = jnp.where(touched, second_step, seconds)
    return (free_new, moments_new, seconds_new, query_grad, up_part, down_part)


def solution(mesh):
    placed = (
        P("query", None),
        P("query", None),
        P("label", None, None),
        P(None, "query"),
        P(None, "query"),
        P("label", None),
        P("label", None),
        P("label", None),
    )
    return jax.shard_map(
        body,
        mesh=mesh,
        in_specs=placed,
        out_specs=(
            P("label", None),
            P("label", None),
            P("label", None),
            P("query", None),
            P("label", "query"),
            P("label", "query"),
        ),
        check_vma=False,
    )
```

profile of v0, /device:TPU:25, one launch (start us, length us, event | category | flops | bytes accessed | tf_op | source)
XLA Modules:
  0.0 643.8 jit_solution(12416014666471665310)
XLA Ops:
  7.2 0.0 copy-start
  7.2 0.0 all-reduce.6.cloned.1.call-start
  7.2 1.0 copy-done
  8.2 0.0 copy-start.2
  8.2 6.1 convert_reduce_fusion.1
  14.4 0.0 copy-start.8
  14.4 0.0 copy-done.2
  14.4 1.3 fusion.16
  15.7 0.0 all-reduce.6.cloned.1.call-update
  15.7 0.0 all-reduce.8.cloned.1.call-start
  15.8 2.9 convert_reduce_fusion
  18.7 0.0 copy-done.8
  18.7 75.3 %all-reduce.6.cloned.1.call-done = f32[64,768]{1,0:T(8,128)} async-done(((f32[64,768]{1,0:T(8,128)}), f32[64,768]{1,0:T(8,128)}) %all-reduce.6.cloned.1.call-update) | async-done | bytes 196624 | tf_op jit(solution)/shard_map/psum | solution.py:32
  94.0 0.0 copy-done.5
  94.0 1.0 add_convert_fusion
  95.0 0.0 copy-done.4
  95.0 0.2 convolution_bitcast_fusion.1
  95.2 0.1 select_reduce_fusion.1
  95.3 235.5 %psum.37 = f32[192,10]{0,1:T(8,128)S(1)} all-reduce(f32[192,10]{0,1:T(8,128)S(1)} %select_reduce_fusion.1), channel_id=1, replica_groups=mesh['label'=64,'query'=8] {'label'}, use_global_device_ids=true, to_apply=%region_5.0 | all-reduce | flops 1920 | bytes 15360 | tf_op jit(solution)/shard_map/psum | solution.py:42
  330.9 0.1 fusion.27
  330.9 0.2 convert_reduce_fusion.2
  331.2 0.1 copy.31
  331.3 0.9 fusion.32
  332.2 0.0 all-reduce.8.cloned.1.call-update
  332.2 0.0 all-reduce.10.cloned.1.call-start
  332.3 1.0 fusion.31
  333.3 83.8 %all-reduce.8.cloned.1.call-done = f32[64,768]{1,0:T(8,128)} async-done(((f32[64,768]{1,0:T(8,128)}), f32[64,768]{1,0:T(8,128)}) %all-reduce.8.cloned.1.call-update) | async-done | bytes 196624 | tf_op jit(solution)/shard_map/psum | solution.py:53
  417.1 1.3 convolution_multiply_fusion
  418.4 3.6 fusion.6
  422.0 0.0 copy-done.1
  422.0 0.0 copy-start.3
  422.0 1.4 convolution_bitcast_fusion
  423.5 0.0 copy-done.3
  423.5 0.7 fusion.14
  424.2 0.0 copy-start.6
  424.2 0.0 copy-start.7
  424.2 1.5 pad_maximum_fusion
  425.7 0.0 all-reduce.10.cloned.1.call-update
  425.7 1.3 dynamic-slice
  427.7 12.6 %psum.35 = f32[64]{0:T(128)S(1)} all-reduce(f32[64]{0:T(128)S(1)} %get-tuple-element.24), channel_id=1, replica_groups=mesh['label'=64,'query'=8] {'query'}, use_global_device_ids=true, to_apply=%region_1.0 | all-reduce | flops 64 | bytes 512 | tf_op jit(solution)/shard_map/psum | solution.py:53
  440.3 0.0 copy-done.6
  440.3 0.0 copy-done.7
  440.3 1.0 fusion.13
  441.3 191.3 %all-reduce.10.cloned.1.call-done = (f32[192,768]{1,0:T(8,128)}, f32[768,768]{0,1:T(8,128)}) async-done(((f32[192,768]{1,0:T(8,128)}, f32[768,768]{0,1:T(8,128)}), (f32[192,768]{1,0:T(8,128)}, f32[768,768]{0,1:T(8,128)})) %all-reduce.10.cloned.1.call-update) | async-done | bytes 2949136 | tf_op jit(solution)/shard_map/psum | solution.py:50
  632.7 1.3 fusion.30
  633.9 0.7 copy.20
  634.7 0.7 copy.21
  635.4 1.9 copy.41
  (8 shorter events, 0.1 us)
Async XLA Ops:
  7.2 1.1 copy-start
  7.2 86.8 %all-reduce.6.cloned.1.call-start = ((), (), s32[]{:S(2)}) async-start(), calls=%async_computation | async-start | bytes 393216 | tf_op jit(solution)/shard_map/psum | solution.py:32
  8.2 6.1 copy-start.2
  14.4 4.3 copy-start.8
  14.4 79.7 %copy-start.5 = (f32[64,768]{1,0:T(8,128)S(1)}, f32[64,768]{1,0:T(8,128)}, u32[]{:S(2)}) copy-start(f32[64,768]{1,0:T(8,128)} %param.13) | copy-start | bytes 589828
  14.4 80.6 %copy-start.4 = (bf16[192,768]{1,0:T(8,128)(2,1)S(1)}, bf16[192,768]{1,0:T(8,128)(2,1)}, u32[]{:S(2)}) copy-start(bf16[192,768]{1,0:T(8,128)(2,1)} %param.8) | copy-start | bytes 884740
  15.7 401.4 %all-reduce.8.cloned.1.call-start = ((), (), s32[]{:S(2)}) async-start(), calls=%async_computation.1 | async-start | bytes 393216 | tf_op jit(solution)/shard_map/psum | solution.py:53
  332.2 300.4 %all-reduce.10.cloned.1.call-start = ((), (), s32[]{:S(2)}) async-start(), calls=%async_computation.2 | async-start | bytes 5898240 | tf_op jit(solution)/shard_map/psum | solution.py:50
  417.1 4.9 copy-start.1
  422.0 1.5 copy-start.3
  424.2 16.2 %copy-start.6 = (f32[64,768]{1,0:T(8,128)S(1)}, f32[64,768]{1,0:T(8,128)}, u32[]{:S(2)}) copy-start(f32[64,768]{1,0:T(8,128)} %param.15) | copy-start | bytes 589828
  424.2 16.2 %copy-start.7 = (f32[64,768]{1,0:T(8,128)S(1)}, f32[64,768]{1,0:T(8,128)}, u32[]{:S(2)}) copy-start(f32[64,768]{1,0:T(8,128)} %param.14) | copy-start | bytes 589828
Sparse Core Ops, SparseCore 0:
  15.8 78.1 all-reduce.5
  332.3 84.7 all-reduce.7
  425.9 206.7 all-reduce.9
where the time goes:
time: 644 us
  waiting for transfers between devices  351 us (55%)
  blocking collectives  248 us (39%)
  between operations  14.6 us (2%)
  matrix products  13 us (2%)
  other arithmetic  10.4 us (2%)
  local copies, waits for them, and re-layouts  7.07 us (1%)
    psum x1, blocking collectives, body(): scores = lax.psum(partial_value, 'label') * temper  235 us
    psum x1, waiting for transfers between devices, body(): query_grad = lax.psum(query_terms, 'label')  191 us
    psum x1, waiting for transfers between devices, body(): label_grad, counts = lax.psum((grad_part, count_part), 'query')  83.8 us
    psum x1, waiting for transfers between devices, body(): encoded = lax.psum(encoded_part, 'query')  75.3 us
  transfers between devices with their start and end apart: 3, of which 3 were waited for; matrix products, arithmetic and copies ran while one was open for 1% of the time, Pallas kernels for 0%

commit v1 on v0

--- a/solution.py
+++ b/solution.py
@@ -29,7 +29,9 @@
     encoded_part = jnp.einsum(
         "lf,df->ld", pooled_hidden, down_weight.astype(jnp.float32), precision=lax.Precision.HIGHEST
     )
-    encoded = lax.psum(encoded_part, "query")
+    encoded = encoded_part
+    for hop in (1, 2, 4):
+        encoded = encoded + lax.ppermute(encoded, "query", [(dev, dev ^ hop) for dev in range(8)])
     label_vec = pooled_text + encoded + free_vectors
     label_bf = label_vec.astype(jnp.bfloat16)
     first_label = lax.axis_index("label") * label_rows

time: 644 us -> 603 us (0.936)
  waiting for transfers between devices: 351 us -> 295 us
  starting transfers between devices: 0.12 us -> 17.9 us
    psum x1 -> x0, waiting for transfers between devices: 75.3 us -> none  [body(): encoded = lax.psum(encoded_part, 'query')]
    ppermute x0 -> x3, starting transfers between devices: none -> 17.8 us  [body(): lax.ppermute(encoded, 'query', [(dev, dev ^ hop) for dev in range(8)])]
    ppermute x0 -> x3, waiting for transfers between devices: none -> 17 us  [body(): lax.ppermute(encoded, 'query', [(dev, dev ^ hop) for dev in range(8)])]
  transfers between devices with their start and end apart: 3 -> 5, of which waited for: 3 -> 5; matrix products, arithmetic and copies ran while one was open for 1% -> 1% of each run, Pallas kernels for 0% -> 0%
where the time goes in v1:
time: 603 us; the launch traced here: 602 us
  waiting for transfers between devices  295 us (49%)
  blocking collectives  246 us (41%)
  starting transfers between devices  17.9 us (3%)
  between operations  14.9 us (2%)
  matrix products  12.3 us (2%)
  other arithmetic  9.56 us (2%)
  local copies, waits for them, and re-layouts  7.07 us (1%)
    psum x1, blocking collectives, body(): scores = lax.psum(partial_value, 'label') * temper  233 us
    psum x1, waiting for transfers between devices, body(): query_grad = lax.psum(query_terms, 'label')  191 us
    psum x1, waiting for transfers between devices, body(): label_grad, counts = lax.psum((grad_part, count_part), 'query')  86.7 us
    ppermute x3, starting transfers between devices, body(): lax.ppermute(encoded, 'query', [(dev, dev ^ hop) for dev in range(8)])  17.8 us
    ppermute x3, waiting for transfers between devices, body(): lax.ppermute(encoded, 'query', [(dev, dev ^ hop) for dev in range(8)])  17 us
    psum x1, blocking collectives, body(): label_grad, counts = lax.psum((grad_part, count_part), 'query')  12.6 us
  transfers between devices with their start and end apart: 5, of which 5 were waited for; matrix products, arithmetic and copies ran while one was open for 1% of the time, Pallas kernels for 0%

profile of v1, /device:TPU:25, one launch (start us, length us, event | category | flops | bytes accessed | tf_op | source)
XLA Modules:
  0.0 602.1 jit_solution(14149343054252642478)
XLA Ops:
  7.2 0.0 copy-start
  7.2 0.0 all-reduce.5.cloned.1.call-start
  7.2 1.0 copy-done
  8.2 6.1 %convert_reduce_fusion.1 = (f32[64,384]{1,0:T(8,128)S(1)}, f32[2048,384]{1,0:T(8,128)}) fusion(bf16[2048,768]{1,0:T(8,128)(2,1)} %bitcast.40, bf16[768,384]{1,0:T(8,128)(2,1)S(1)} %copy-done), kind=kOutput, calls=%fused_computation.15 | convolution fusion | flops 1216585728 | bytes 6979584 | tf_op jit(solution)/shard_map/dot_general | solution.py:23
  14.4 0.0 copy-done.2
  14.4 0.6 fusion.16
  15.0 4.0 collective-permute-start
  19.0 4.6 collective-permute-done
  23.7 5.8 collective-permute-start.1
  29.5 2.9 convert_reduce_fusion
  32.4 5.8 collective-permute-done.1
  38.2 8.0 %collective-permute-start.2 = (f32[64,768]{1,0:T(8,128)S(1)}, f32[64,768]{1,0:T(8,128)S(1)}, u32[]{:S(2)}, u32[]{:S(2)}) collective-permute-start(f32[64,768]{1,0:T(8,128)S(1)} %add.49), channel_id=1, source_target_pairs={{0,4},{1,5},{2,6},{3,7},{4,0},{5,1},{6,2},{7,3},{8,12},{9,13},{10,... | collective-permute-start | bytes 589832 | tf_op jit(solution)/shard_map/ppermute | solution.py:34
  46.2 0.0 copy-done.8
  46.2 6.6 %collective-permute-done.2 = f32[64,768]{1,0:T(8,128)S(1)} collective-permute-done((f32[64,768]{1,0:T(8,128)S(1)}, f32[64,768]{1,0:T(8,128)S(1)}, u32[]{:S(2)}, u32[]{:S(2)}) %collective-permute-start.2) | collective-permute-done | bytes 196640 | tf_op jit(solution)/shard_map/ppermute | solution.py:34
  52.8 0.0 copy-done.5
  52.8 0.1 add_convert_fusion
  52.9 0.0 copy-done.4
  52.9 0.2 convolution_bitcast_fusion.1
  53.1 0.1 select_reduce_fusion.1
  53.2 233.1 %psum.29 = f32[192,10]{0,1:T(8,128)S(1)} all-reduce(f32[192,10]{0,1:T(8,128)S(1)} %select_reduce_fusion.1), channel_id=1, replica_groups=mesh['label'=64,'query'=8] {'label'}, use_global_device_ids=true, to_apply=%region_4.0 | all-reduce | flops 1920 | bytes 15360 | tf_op jit(solution)/shard_map/psum | solution.py:44
  286.4 0.1 fusion.27
  286.5 0.2 convert_reduce_fusion.2
  286.7 0.1 copy.31
  286.8 0.9 fusion.32
  287.7 0.0 all-reduce.5.cloned.1.call-update
  287.7 0.0 all-reduce.7.cloned.1.call-start
  287.8 1.0 fusion.31
  288.8 86.7 %all-reduce.5.cloned.1.call-done = f32[64,768]{1,0:T(8,128)} async-done(((f32[64,768]{1,0:T(8,128)}), f32[64,768]{1,0:T(8,128)}) %all-reduce.5.cloned.1.call-update) | async-done | bytes 196624 | tf_op jit(solution)/shard_map/psum | solution.py:55
  375.5 1.3 convolution_multiply_fusion
  376.8 3.6 fusion.6
  380.4 0.0 copy-done.1
  380.4 0.0 copy-start.3
  380.4 1.4 convolution_bitcast_fusion
  381.8 0.0 copy-done.3
  381.9 0.7 fusion.14
  382.5 0.0 copy-start.6
  382.5 0.0 copy-start.7
  382.6 1.5 pad_maximum_fusion
  384.1 0.0 all-reduce.7.cloned.1.call-update
  384.1 1.3 dynamic-slice
  386.0 12.6 %psum.28 = f32[64]{0:T(128)S(1)} all-reduce(f32[64]{0:T(128)S(1)} %get-tuple-element.24), channel_id=1, replica_groups=mesh['label'=64,'query'=8] {'query'}, use_global_device_ids=true, to_apply=%region_1.0 | all-reduce | flops 64 | bytes 512 | tf_op jit(solution)/shard_map/psum | solution.py:55
  398.7 0.0 copy-done.6
  398.7 1.0 fusion.13
  399.7 190.9 %all-reduce.7.cloned.1.call-done = (f32[192,768]{1,0:T(8,128)}, f32[768,768]{0,1:T(8,128)}) async-done(((f32[192,768]{1,0:T(8,128)}, f32[768,768]{0,1:T(8,128)}), (f32[192,768]{1,0:T(8,128)}, f32[768,768]{0,1:T(8,128)})) %all-reduce.7.cloned.1.call-update) | async-done | bytes 2949136 | tf_op jit(solution)/shard_map/psum | solution.py:52
  590.6 1.3 fusion.30
  591.9 0.7 copy.20
  592.6 0.7 copy.21
  593.4 1.9 copy.40
  (13 shorter events, 0.1 us)
Async XLA Ops:
  7.2 1.1 copy-start
  7.2 368.3 %all-reduce.5.cloned.1.call-start = ((), (), s32[]{:S(2)}) async-start(), calls=%async_computation | async-start | bytes 393216 | tf_op jit(solution)/shard_map/psum | solution.py:55
  8.2 6.1 %copy-start.2 = (bf16[768,384]{1,0:T(8,128)(2,1)S(1)}, bf16[768,384]{1,0:T(8,128)(2,1)}, u32[]{:S(2)}) copy-start(bf16[768,384]{1,0:T(8,128)(2,1)} %param.12) | copy-start | bytes 1769476
  14.4 31.8 %copy-start.8 = (s32[192,10]{0,1:T(8,128)S(1)}, s32[192,10]{0,1:T(8,128)}, u32[]{:S(2)}) copy-start(s32[192,10]{0,1:T(8,128)} %param.9) | copy-start | bytes 23044
  14.4 38.5 %copy-start.5 = (f32[64,768]{1,0:T(8,128)S(1)}, f32[64,768]{1,0:T(8,128)}, u32[]{:S(2)}) copy-start(f32[64,768]{1,0:T(8,128)} %param.13) | copy-start | bytes 589828
  14.4 38.5 %copy-start.4 = (bf16[192,768]{1,0:T(8,128)(2,1)S(1)}, bf16[192,768]{1,0:T(8,128)(2,1)}, u32[]{:S(2)}) copy-start(bf16[192,768]{1,0:T(8,128)(2,1)} %param.8) | copy-start | bytes 884740
  15.0 8.6 %collective-permute-start = (f32[64,768]{1,0:T(8,128)S(1)}, f32[64,768]{1,0:T(8,128)S(1)}, u32[]{:S(2)}, u32[]{:S(2)}) collective-permute-start(f32[64,768]{1,0:T(8,128)S(1)} %fusion.16), channel_id=1, source_target_pairs={{0,1},{1,0},{2,3},{3,2},{4,5},{5,4},{6,7},{7,6},{8,9},{9,8},{10,11... | collective-permute-start | bytes 589832 | tf_op jit(solution)/shard_map/ppermute | solution.py:34
  23.7 14.5 %collective-permute-start.1 = (f32[64,768]{1,0:T(8,128)S(1)}, f32[64,768]{1,0:T(8,128)S(1)}, u32[]{:S(2)}, u32[]{:S(2)}) collective-permute-start(f32[64,768]{1,0:T(8,128)S(1)} %add.48), channel_id=1, source_target_pairs={{0,2},{1,3},{2,0},{3,1},{4,6},{5,7},{6,4},{7,5},{8,10},{9,11},{10,... | collective-permute-start | bytes 589832 | tf_op jit(solution)/shard_map/ppermute | solution.py:34
  38.2 14.7 %collective-permute-start.2 = (f32[64,768]{1,0:T(8,128)S(1)}, f32[64,768]{1,0:T(8,128)S(1)}, u32[]{:S(2)}, u32[]{:S(2)}) collective-permute-start(f32[64,768]{1,0:T(8,128)S(1)} %add.49), channel_id=1, source_target_pairs={{0,4},{1,5},{2,6},{3,7},{4,0},{5,1},{6,2},{7,3},{8,12},{9,13},{10,... | collective-permute-start | bytes 589832 | tf_op jit(solution)/shard_map/ppermute | solution.py:34
  287.7 302.9 %all-reduce.7.cloned.1.call-start = ((), (), s32[]{:S(2)}) async-start(), calls=%async_computation.1 | async-start | bytes 5898240 | tf_op jit(solution)/shard_map/psum | solution.py:52
  375.5 4.9 copy-start.1
  380.4 1.4 copy-start.3
  382.5 16.2 %copy-start.6 = (f32[64,768]{1,0:T(8,128)S(1)}, f32[64,768]{1,0:T(8,128)}, u32[]{:S(2)}) copy-start(f32[64,768]{1,0:T(8,128)} %param.15) | copy-start | bytes 589828
  382.5 16.2 %copy-start.7 = (f32[64,768]{1,0:T(8,128)S(1)}, f32[64,768]{1,0:T(8,128)}, u32[]{:S(2)}) copy-start(f32[64,768]{1,0:T(8,128)} %param.14) | copy-start | bytes 589828
Sparse Core Ops, SparseCore 0:
  287.8 87.6 all-reduce.4
  384.2 206.3 all-reduce.6
